TPU v7x, 32 devices: a whole 2x2x4 slice. The times are simulated.
32 devices in a mesh: tr: 4 (over z), tc: 8 (over y, x, core).
Axes of the slice: x: 2, y: 2, z: 4, core: 2. Of those that a mesh axis runs over, the one named last changes fastest.
Arguments:
- embeddings: bfloat16 [24576, 1024], P(('tr', 'tc')), may hold values from -100 to 100
- labels: int32 [24576], P(('tr', 'tc')), may hold values from 0 to 15, as said below
Outputs:
- best_sim: float32 [24576], P(('tr', 'tc'))
- weighted: float32 [24576], P(('tr', 'tc'))
- flag: float32 [24576], P(('tr', 'tc'))
Inputs may be any that keep to these rules, and one draw needn't show every extreme that they name: In each aligned block of 768 files (one corpus shard), at most 576 files have labels // 4 equal to any one value g, and every shard has exactly 576 for some g; for every g and every c below 8, the shards c, c + 8, c + 16, ... together hold exactly 768 files with labels // 4 = g; every label is held by two or more files.
All inputs are finite; a program needn't handle non-finite values.
Results may differ from a plain program's by a relative error of at most 0.0013.
Values may be sent and summed in bfloat16 or wider, within the bound.
A program may use at most 128 MiB of HBM per device.

v0:
```python
import jax
import jax.numpy as jnp
from jax import lax
from jax.sharding import PartitionSpec as P

GROUP_CLUSTERS = 4


SCALE = 256.0
NEGATIVE = -1e30
EPSILON = 1e-06
THRESHOLD = 0.3
SHARPNESS = 50.0


def fresh_stats(count):
    return (
        jnp.full((count,), NEGATIVE, jnp.float32),
        jnp.zeros((count,), jnp.float32),
        jnp.zeros((count,), jnp.float32),
    )


def tile_update(stats, sims, mask):
    best, total, weight = stats
    scores = SCALE * sims
    block_top = jnp.max(jnp.where(mask, scores, NEGATIVE), axis=1)
    new_best = jnp.maximum(best, block_top)
    factor = jnp.exp(best - new_best)
    terms = jnp.where(mask, jnp.exp(scores - new_best[:, None]), 0.0)
    return (
        new_best,
        total * factor + jnp.sum(terms, axis=1),
        weight * factor + jnp.sum(terms * sims, axis=1),
    )


def pair_products(left, right):
    return lax.dot_general(
        left, right, (((1,), (1,)), ((), ())), preferred_element_type=jnp.float32
    )


def per_device(embeddings, labels):
    shard_rows, feature_dim = embeddings.shape
    tile_rows = lax.axis_size("tr")
    capacity = 3 * shard_rows // tile_rows
    values = embeddings.astype(jnp.float32)
    unit = (values * lax.rsqrt(jnp.sum(values * values, axis=1, keepdims=True) + EPSILON)).astype(
        jnp.bfloat16
    )
    owner = labels // GROUP_CLUSTERS
    onehot = (owner[:, None] == jnp.arange(tile_rows, dtype=jnp.int32)[None, :]).astype(jnp.int32)
    ranks = jnp.sum((jnp.cumsum(onehot, axis=0) - 1) * onehot, axis=1)
    slots = owner * capacity + ranks
    send_rows = jnp.zeros((tile_rows * capacity, feature_dim), jnp.bfloat16).at[slots].set(unit)
    send_labels = jnp.full((tile_rows * capacity,), -1, jnp.int32).at[slots].set(labels)
    got_rows, got_labels = (
        lax.all_to_all(
            send_rows.reshape(tile_rows, capacity, feature_dim),
            "tr",
            split_axis=0,
            concat_axis=0,
            tiled=True,
        ),
        lax.all_to_all(
            send_labels.reshape(tile_rows, capacity), "tr", split_axis=0, concat_axis=0, tiled=True
        ),
    )
    flat_rows = got_rows.reshape(tile_rows * capacity, feature_dim)
    flat_labels = got_labels.reshape(tile_rows * capacity)
    filled = flat_labels >= 0
    position = jnp.cumsum(filled.astype(jnp.int32)) - 1
    target = jnp.where(filled, position, shard_rows)
    queries = (
        jnp.zeros((shard_rows, feature_dim), jnp.bfloat16).at[target].set(flat_rows, mode="drop")
    )
    query_labels = jnp.zeros((shard_rows,), jnp.int32).at[target].set(flat_labels, mode="drop")
    local_range = jnp.arange(shard_rows, dtype=jnp.int32)
    query_index = lax.axis_index("tc") * shard_rows + local_range
    stats = fresh_stats(shard_rows)
    key_rows = lax.all_gather(queries, "tc", axis=0, tiled=True)
    key_labels = lax.all_gather(query_labels, "tc", axis=0, tiled=True)
    count = key_rows.shape[0] // shard_rows
    offsets = jnp.arange(count, dtype=jnp.int32) * shard_rows

    def step(inner, item):
        block_rows, block_labels, offset = item
        sims = pair_products(queries, block_rows)
        mask = (query_labels[:, None] == block_labels[None, :]) & (
            query_index[:, None] != offset + local_range[None, :]
        )
        return (tile_update(inner, sims, mask), None)

    stats, unused = lax.scan(
        step,
        stats,
        (
            key_rows.reshape(count, shard_rows, feature_dim),
            key_labels.reshape(count, shard_rows),
            offsets,
        ),
    )
    best_sim = stats[0] / SCALE
    weighted = stats[2] / stats[1]
    flag = jax.nn.sigmoid(SHARPNESS * (best_sim - THRESHOLD))
    results = jnp.stack([best_sim, weighted, flag])
    spread = jnp.where(filled[None, :], results[:, jnp.where(filled, position, 0)], 0.0)
    back = lax.all_to_all(
        spread.reshape(3, tile_rows, capacity), "tr", split_axis=1, concat_axis=1, tiled=True
    )
    mine = back.reshape(3, tile_rows * capacity)[:, slots]
    return (mine[0], mine[1], mine[2])


def solution(mesh):
    placed = (P(("tr", "tc"), None), P(("tr", "tc")))
    return jax.shard_map(
        per_device,
        mesh=mesh,
        in_specs=placed,
        out_specs=(P(("tr", "tc")), P(("tr", "tc")), P(("tr", "tc"))),
        check_vma=False,
    )
```

profile of v0, /device:TPU:0, one launch (start us, length us, event | category | flops | bytes accessed | tf_op | source)
XLA Modules:
  0.0 301.3 jit_solution(6147068701563966140)
XLA Ops:
  10.4 3.5 %scatter_custom_fusion = s32[2304]{0:T(1024)S(1)} fusion(s32[768]{0:T(1024)S(1)} %compare_select_fusion.2, s32[768]{0:T(1024)} %param.5, s32[]{:T(128)} %constant.30.clone.1), kind=kCustom, calls=%fused_computation.67 | custom fusion | bytes 9728 | tf_op jit(solution)/shard_map/scatter | solution.py:57
  14.6 6.3 %all-to-all-start = ((s32[4,1,576]{2,1,0:T(1,128)}), s32[4,1,576]{2,1,0:T(1,128)S(1)}, u32[]{:S(2)}, u32[]{:S(2)}) async-start(s32[4,1,576]{2,1,0:T(1,128)} %all_to_all.12), calls=%async_computation | async-start | bytes 20480 | tf_op jit(solution)/shard_map/all_to_all | solution.py:66
  20.9 1.8 fusion.12
  22.7 9.3 %scatter_custom_fusion.2 = bf16[2304,1024]{1,0:T(8,128)(2,1)} fusion(s32[768]{0:T(1024)S(1)} %compare_select_fusion.2, bf16[]{:T(256)} %constant.72.clone.1, bf16[768,1024]{1,0:T(8,128)(2,1)S(1)} %copy-done, f32[768]{0:T(1024)S(1)} %add_rsqrt_fusion), kind=kCustom, calls=%fused_computation.32 | custom fusion | flops 2359296 | bytes 6295554 | tf_op jit(solution)/shard_map/scatter | solution.py:56
  32.0 5.1 %all-to-all-start.1 = ((bf16[4,576,1024]{2,1,0:T(8,128)(2,1)}), bf16[4,576,1024]{2,1,0:T(8,128)(2,1)}, u32[]{:S(2)}, u32[]{:S(2)}) async-start(bf16[4,576,1024]{2,1,0:T(8,128)(2,1)} %bitcast.76), calls=%async_computation.1 | async-start | bytes 9437184 | tf_op jit(solution)/shard_map/all_to_all | solution.py:59
  38.0 103.3 %all-to-all-done.1 = bf16[4,576,1024]{2,1,0:T(8,128)(2,1)} async-done(((bf16[4,576,1024]{2,1,0:T(8,128)(2,1)}), bf16[4,576,1024]{2,1,0:T(8,128)(2,1)}, u32[]{:S(2)}, u32[]{:S(2)}) %all-to-all-start.1) | async-done | bytes 4718624 | tf_op jit(solution)/shard_map/all_to_all | solution.py:59
  141.4 15.1 %scatter_custom_fusion.3 = bf16[768,1024]{1,0:T(8,128)(2,1)} fusion(s32[2304]{0:T(1024)S(1)} %get-tuple-element.109, bf16[2304,1024]{1,0:T(8,128)(2,1)} %bitcast.3, bf16[]{:T(256)} %constant.72.clone.1), kind=kCustom, calls=%fused_computation.35 | custom fusion | bytes 1573376 | tf_op jit(solution)/shard_map/scatter | solution.py:76
  156.6 9.0 %scatter_custom_fusion.1 = s32[768]{0:T(1024)S(1)} fusion(s32[2304]{0:T(1024)S(1)} %get-tuple-element.109, s32[2304]{0:T(1024)S(1)} %reshape.203, s32[]{:T(128)} %constant.33.clone.1), kind=kCustom, calls=%fused_computation.77 | custom fusion | bytes 3076 | tf_op jit(solution)/shard_map/scatter | solution.py:78
  165.6 9.1 %all-gather = s32[8,1,768]{2,1,0:T(1,128)S(1)} all-gather(s32[1,1,768]{2,1,0:T(1,128)S(1)} %reshape.226), channel_id=1, replica_groups=mesh['tr'=4,'tc'=8] {'tc'}, dimensions={0}, use_global_device_ids=true | all-gather | bytes 27648 | tf_op jit(solution)/shard_map/all_gather | solution.py:83
  174.8 53.2 %all-gather.3.cloned.1.call-done = bf16[6144,1024]{1,0:T(8,128)(2,1)} async-done(((bf16[768,1024]{1,0:T(8,128)(2,1)}), bf16[6144,1024]{1,0:T(8,128)(2,1)}) %all-gather.3.cloned.1.call-update) | async-done | bytes 12582928 | tf_op jit(solution)/shard_map/all_gather | solution.py:82
  228.0 47.8 %while.15 = (s32[]{:T(128)}, f32[768]{0:T(1024)S(1)}, f32[768]{0:T(1024)S(1)}, f32[768]{0:T(1024)S(1)}, s32[768]{0:T(1024)S(1)}, /*index=5*/s32[8,768]{1,0:T(8,1...) while((s32[]{:T(128)}, f32[768]{0:T(1024)S(1)}, ...), condition=%wide.region_14.15_spmd.clone, body=%wide.region_10.14_spmd.clone.sunk | while | flops 1216813824 | bytes 7953572 | solution.py:95
  229.2 3.5 %select_reduce_fusion.2 = (f32[768]{0:T(1024)S(1)}, f32[768,768]{1,0:T(8,128)S(1)}) fusion(s32[768]{0:T(1024)S(1)} %get-tuple-element.213, s32[768]{0:T(1024)S(1)} %get-tuple-element.249, s32[768]{0:T(1024)S(1)} %get-tuple-element.214, s32[768]{0:T(1024)S(1)} %dynamic-slice_reduce_fusion.2, bf16[768,1024]{1,0:T(8,128)(2,1)} %get-tuple-element.253, ...), kind=kOutput, calls=%fused_computation.12.clone.1 | convolution fusion | flops 1211497728 | bytes 5520388 | tf_op jit(solution)/shard_map/while/body/eval_jaxpr/dot_general | solution.py:39
  235.2 3.5 %select_reduce_fusion.2 = (f32[768]{0:T(1024)S(1)}, f32[768,768]{1,0:T(8,128)S(1)}) fusion(s32[768]{0:T(1024)S(1)} %get-tuple-element.213, s32[768]{0:T(1024)S(1)} %get-tuple-element.249, s32[768]{0:T(1024)S(1)} %get-tuple-element.214, s32[768]{0:T(1024)S(1)} %dynamic-slice_reduce_fusion.2, bf16[768,1024]{1,0:T(8,128)(2,1)} %get-tuple-element.253, ...), kind=kOutput, calls=%fused_computation.12.clone.1 | convolution fusion | flops 1211497728 | bytes 5520388 | tf_op jit(solution)/shard_map/while/body/eval_jaxpr/dot_general | solution.py:39
  241.2 3.5 %select_reduce_fusion.2 = (f32[768]{0:T(1024)S(1)}, f32[768,768]{1,0:T(8,128)S(1)}) fusion(s32[768]{0:T(1024)S(1)} %get-tuple-element.213, s32[768]{0:T(1024)S(1)} %get-tuple-element.249, s32[768]{0:T(1024)S(1)} %get-tuple-element.214, s32[768]{0:T(1024)S(1)} %dynamic-slice_reduce_fusion.2, bf16[768,1024]{1,0:T(8,128)(2,1)} %get-tuple-element.253, ...), kind=kOutput, calls=%fused_computation.12.clone.1 | convolution fusion | flops 1211497728 | bytes 5520388 | tf_op jit(solution)/shard_map/while/body/eval_jaxpr/dot_general | solution.py:39
  247.2 3.5 %select_reduce_fusion.2 = (f32[768]{0:T(1024)S(1)}, f32[768,768]{1,0:T(8,128)S(1)}) fusion(s32[768]{0:T(1024)S(1)} %get-tuple-element.213, s32[768]{0:T(1024)S(1)} %get-tuple-element.249, s32[768]{0:T(1024)S(1)} %get-tuple-element.214, s32[768]{0:T(1024)S(1)} %dynamic-slice_reduce_fusion.2, bf16[768,1024]{1,0:T(8,128)(2,1)} %get-tuple-element.253, ...), kind=kOutput, calls=%fused_computation.12.clone.1 | convolution fusion | flops 1211497728 | bytes 5520388 | tf_op jit(solution)/shard_map/while/body/eval_jaxpr/dot_general | solution.py:39
  253.1 3.5 %select_reduce_fusion.2 = (f32[768]{0:T(1024)S(1)}, f32[768,768]{1,0:T(8,128)S(1)}) fusion(s32[768]{0:T(1024)S(1)} %get-tuple-element.213, s32[768]{0:T(1024)S(1)} %get-tuple-element.249, s32[768]{0:T(1024)S(1)} %get-tuple-element.214, s32[768]{0:T(1024)S(1)} %dynamic-slice_reduce_fusion.2, bf16[768,1024]{1,0:T(8,128)(2,1)} %get-tuple-element.253, ...), kind=kOutput, calls=%fused_computation.12.clone.1 | convolution fusion | flops 1211497728 | bytes 5520388 | tf_op jit(solution)/shard_map/while/body/eval_jaxpr/dot_general | solution.py:39
  259.1 3.5 %select_reduce_fusion.2 = (f32[768]{0:T(1024)S(1)}, f32[768,768]{1,0:T(8,128)S(1)}) fusion(s32[768]{0:T(1024)S(1)} %get-tuple-element.213, s32[768]{0:T(1024)S(1)} %get-tuple-element.249, s32[768]{0:T(1024)S(1)} %get-tuple-element.214, s32[768]{0:T(1024)S(1)} %dynamic-slice_reduce_fusion.2, bf16[768,1024]{1,0:T(8,128)(2,1)} %get-tuple-element.253, ...), kind=kOutput, calls=%fused_computation.12.clone.1 | convolution fusion | flops 1211497728 | bytes 5520388 | tf_op jit(solution)/shard_map/while/body/eval_jaxpr/dot_general | solution.py:39
  265.1 3.5 %select_reduce_fusion.2 = (f32[768]{0:T(1024)S(1)}, f32[768,768]{1,0:T(8,128)S(1)}) fusion(s32[768]{0:T(1024)S(1)} %get-tuple-element.213, s32[768]{0:T(1024)S(1)} %get-tuple-element.249, s32[768]{0:T(1024)S(1)} %get-tuple-element.214, s32[768]{0:T(1024)S(1)} %dynamic-slice_reduce_fusion.2, bf16[768,1024]{1,0:T(8,128)(2,1)} %get-tuple-element.253, ...), kind=kOutput, calls=%fused_computation.12.clone.1 | convolution fusion | flops 1211497728 | bytes 5520388 | tf_op jit(solution)/shard_map/while/body/eval_jaxpr/dot_general | solution.py:39
  271.0 3.5 %select_reduce_fusion.2 = (f32[768]{0:T(1024)S(1)}, f32[768,768]{1,0:T(8,128)S(1)}) fusion(s32[768]{0:T(1024)S(1)} %get-tuple-element.213, s32[768]{0:T(1024)S(1)} %get-tuple-element.249, s32[768]{0:T(1024)S(1)} %get-tuple-element.214, s32[768]{0:T(1024)S(1)} %dynamic-slice_reduce_fusion.2, bf16[768,1024]{1,0:T(8,128)(2,1)} %get-tuple-element.253, ...), kind=kOutput, calls=%fused_computation.12.clone.1 | convolution fusion | flops 1211497728 | bytes 5520388 | tf_op jit(solution)/shard_map/while/body/eval_jaxpr/dot_general | solution.py:39
  276.0 3.9 %gather_fusion = f32[2304,3]{1,0:T(8,128)S(1)} fusion(f32[3,768]{0,1:T(8,128)S(1)} %copy.11, s32[3072]{0:T(1024)S(1)} %pad_clamp_fusion), kind=kCustom, calls=%fused_computation | custom fusion | bytes 64512 | tf_op jit(solution)/shard_map/gather | solution.py:108
  281.0 4.6 %all-to-all-start.2 = ((f32[3,4,576]{2,0,1:T(4,128)}), f32[3,4,576]{2,0,1:T(4,128)S(1)}, u32[]{:S(2)}, u32[]{:S(2)}) async-start(f32[3,4,576]{2,0,1:T(4,128)} %broadcast_select_fusion), calls=%async_computation.2 | async-start | bytes 81920 | tf_op jit(solution)/shard_map/all_to_all | solution.py:109
  285.6 5.7 %all-to-all-done.2 = f32[3,4,576]{2,0,1:T(4,128)S(1)} async-done(((f32[3,4,576]{2,0,1:T(4,128)}), f32[3,4,576]{2,0,1:T(4,128)S(1)}, u32[]{:S(2)}, u32[]{:S(2)}) %all-to-all-start.2) | async-done | bytes 27680 | tf_op jit(solution)/shard_map/all_to_all | solution.py:109
  291.6 1.6 gather_fusion.1
  293.2 1.2 slice_reduce_fusion
  (101 shorter events, 25.9 us)
Async XLA Ops:
  7.2 15.5 %copy-start = (bf16[768,1024]{1,0:T(8,128)(2,1)S(1)}, bf16[768,1024]{1,0:T(8,128)(2,1)}, u32[]{:S(2)}) copy-start(bf16[768,1024]{1,0:T(8,128)(2,1)} %param.4) | copy-start | bytes 4718596
  14.6 17.4 %all-to-all-start = ((s32[4,1,576]{2,1,0:T(1,128)}), s32[4,1,576]{2,1,0:T(1,128)S(1)}, u32[]{:S(2)}, u32[]{:S(2)}) async-start(s32[4,1,576]{2,1,0:T(1,128)} %all_to_all.12), calls=%async_computation | async-start | bytes 20480 | tf_op jit(solution)/shard_map/all_to_all | solution.py:66
  32.0 109.4 %all-to-all-start.1 = ((bf16[4,576,1024]{2,1,0:T(8,128)(2,1)}), bf16[4,576,1024]{2,1,0:T(8,128)(2,1)}, u32[]{:S(2)}, u32[]{:S(2)}) async-start(bf16[4,576,1024]{2,1,0:T(8,128)(2,1)} %bitcast.76), calls=%async_computation.1 | async-start | bytes 9437184 | tf_op jit(solution)/shard_map/all_to_all | solution.py:59
  37.1 190.9 %all-gather.3.cloned.1.call-start = ((), (), s32[]{:S(2)}) async-start(), calls=%async_computation.3 | async-start | bytes 14155776 | tf_op jit(solution)/shard_map/all_gather | solution.py:82
  281.0 10.3 %all-to-all-start.2 = ((f32[3,4,576]{2,0,1:T(4,128)}), f32[3,4,576]{2,0,1:T(4,128)S(1)}, u32[]{:S(2)}, u32[]{:S(2)}) async-start(f32[3,4,576]{2,0,1:T(4,128)} %broadcast_select_fusion), calls=%async_computation.2 | async-start | bytes 81920 | tf_op jit(solution)/shard_map/all_to_all | solution.py:109
Sparse Core Ops, SparseCore 0:
  156.6 71.3 all-gather.2
where the time goes:
time: 302 us; the launch traced here: 301 us
  waiting for transfers between devices  162 us (54%)
  local copies, waits for them, and re-layouts  41.5 us (14%)
  other arithmetic  29.7 us (10%)
  matrix products  28 us (9%)
  starting transfers between devices  16 us (5%)
  between operations  14.2 us (5%)
  blocking collectives  9.12 us (3%)
    all_to_all x1, waiting for transfers between devices, per_device(): lax.all_to_all(send_rows.reshape(tile_rows, capacity, feature_dim), 'tr',...  103 us
    all_gather x1, waiting for transfers between devices, per_device(): key_rows = lax.all_gather(queries, 'tc', axis=0, tiled=True)  53.2 us
    dot_general x8, matrix products, pair_products(): lax.dot_general(left, right, (((1,), (1,)), ((), ())), preferred_element_...  28 us
    scatter x1, local copies, waits for them, and re-layouts, per_device(): jnp.zeros((shard_rows, feature_dim), jnp.bfloat16).at[target]  15.1 us
    scatter x1, other arithmetic, per_device(): jnp.zeros((tile_rows * capacity, feature_dim), jnp.bfloat16).at[slots]  9.27 us
    reduce_sum x8, other arithmetic, tile_update(): jnp.sum(terms * sims, axis=1)  9.12 us
    all_gather x1, blocking collectives, per_device(): key_labels = lax.all_gather(query_labels, 'tc', axis=0, tiled=True)  9.12 us
    scatter x1, local copies, waits for them, and re-layouts, per_device(): jnp.zeros((shard_rows,), jnp.int32).at[target].set(flat_labels, mode='drop')  8.97 us
  transfers between devices with their start and end apart: 4, of which 3 were waited for; matrix products, arithmetic and copies ran while one was open for 7% of the time, Pallas kernels for 0%

commit v1 on v0

v1 whole, which is shorter than its diff:
```python
import functools

import jax
import jax.numpy as jnp
from jax import lax
from jax.experimental import pallas as pl
from jax.experimental.pallas import tpu as pltpu
from jax.sharding import PartitionSpec as P

GROUP_CLUSTERS = 4


SCALE = 256.0
NEGATIVE = -1e30
EPSILON = 1e-06
THRESHOLD = 0.3
SHARPNESS = 50.0
TILE = 256
CHUNKS = 2


def stats_kernel(chunks, q_lo, q_hi, k_lo, k_hi, place, q_labels, k_labels, *refs):
    queries, keys = refs[:chunks], refs[chunks : 2 * chunks]
    best_ref, weighted_ref, sims_ref, top_ref = refs[2 * chunks :]
    block = pl.program_id(0)
    rows = queries[0].shape[0]
    tiles = rows // TILE

    @pl.when(block == 0)
    def _():
        top_ref[...] = jnp.full(top_ref.shape, NEGATIVE, jnp.float32)

    for kt in range(tiles):
        kn = block * tiles + kt
        for qt in range(tiles):
            own = block == place[0]
            q_rows = pl.ds(qt * TILE, TILE)
            k_rows = pl.ds(kt * TILE, TILE)

            @pl.when((q_lo[qt] <= k_hi[kn]) & (k_lo[kn] <= q_hi[qt]))
            def _():
                sims = None
                for c in range(chunks):
                    part = lax.dot_general(
                        queries[c][q_rows, :],
                        keys[c][k_rows, :],
                        (((1,), (1,)), ((), ())),
                        preferred_element_type=jnp.float32,
                    )
                    sims = part if sims is None else sims + part
                mask = q_labels[q_rows, :] == k_labels[0, :, k_rows]
                if qt == kt:
                    row = lax.broadcasted_iota(jnp.int32, (TILE, TILE), 0)
                    col = lax.broadcasted_iota(jnp.int32, (TILE, TILE), 1)
                    mask = mask & ((row != col) | jnp.logical_not(own))
                sims = jnp.where(mask, sims, NEGATIVE)
                sims_ref[kn, q_rows, :] = sims
                part = jnp.maximum(sims[:, :128], sims[:, 128:])
                top_ref[q_rows, :] = jnp.maximum(top_ref[q_rows, :], part)

    @pl.when(block == pl.num_programs(0) - 1)
    def _():
        for qt in range(tiles):
            q_rows = pl.ds(qt * TILE, TILE)
            best = jnp.max(top_ref[q_rows, :], axis=1, keepdims=True)

            def step(kn, carry):
                def visit(carry):
                    total, weight = carry
                    sims = sims_ref[kn, q_rows, :]
                    terms = jnp.exp(SCALE * (sims - best))
                    both = terms * sims
                    return (
                        total + (terms[:, :128] + terms[:, 128:]),
                        weight + (both[:, :128] + both[:, 128:]),
                    )

                meets = (q_lo[qt] <= k_hi[kn]) & (k_lo[kn] <= q_hi[qt])
                return lax.cond(meets, visit, lambda same: same, carry)

            zero = jnp.zeros((TILE, 128), jnp.float32)
            total, weight = lax.fori_loop(0, sims_ref.shape[0], step, (zero, zero))
            best_ref[q_rows, :] = best
            weighted_ref[q_rows, :] = jnp.sum(weight, axis=1, keepdims=True) / jnp.sum(
                total, axis=1, keepdims=True
            )


def cluster_stats(queries, keys, query_labels, key_labels, place):
    chunks = len(queries)
    rows, width = queries[0].shape
    members = keys[0].shape[0]
    q_tiles = query_labels.reshape(-1, TILE)
    k_tiles = key_labels.reshape(-1, TILE)
    smem = pl.BlockSpec(memory_space=pltpu.SMEM)
    scratch = rows * members * 4
    best, weighted = pl.pallas_call(
        functools.partial(stats_kernel, chunks),
        grid=(members // rows,),
        in_specs=[smem] * 5
        + [
            pl.BlockSpec((rows, 1), lambda b: (0, 0)),
            pl.BlockSpec((1, 1, rows), lambda b: (b, 0, 0)),
        ]
        + [pl.BlockSpec((rows, width), lambda b: (0, 0))] * chunks
        + [pl.BlockSpec((rows, width), lambda b: (b, 0))] * chunks,
        out_specs=[pl.BlockSpec((rows, 1), lambda b: (0, 0))] * 2,
        out_shape=[jax.ShapeDtypeStruct((rows, 1), jnp.float32)] * 2,
        scratch_shapes=[
            pltpu.VMEM((members // TILE, rows, TILE), jnp.float32),
            pltpu.VMEM((rows, 128), jnp.float32),
        ],
        compiler_params=pltpu.CompilerParams(vmem_limit_bytes=scratch + (16 << 20)),
        cost_estimate=pl.CostEstimate(
            flops=2 * rows * members * width * chunks,
            bytes_accessed=2 * members * width * chunks,
            transcendentals=rows * members,
        ),
    )(
        q_tiles[:, 0],
        q_tiles[:, -1],
        k_tiles[:, 0],
        k_tiles[:, -1],
        place.reshape(1),
        query_labels[:, None],
        key_labels.reshape(-1, 1, rows),
        *queries,
        *keys,
    )
    return best[:, 0], weighted[:, 0]


def permute(target, count, parts):
    matrix = (jnp.arange(count, dtype=jnp.int32)[:, None] == target[None, :]).astype(jnp.bfloat16)
    return [
        jnp.dot(matrix, part, preferred_element_type=jnp.float32).astype(jnp.bfloat16)
        for part in parts
    ]


def exclusive(values, axis):
    return jnp.cumsum(values, axis=axis) - values


def per_device(embeddings, labels):
    shard_rows, feature_dim = embeddings.shape
    tile_rows = lax.axis_size("tr")
    columns = lax.axis_size("tc")
    me = lax.axis_index("tr")
    place = lax.axis_index("tc")
    clusters = tile_rows * GROUP_CLUSTERS
    share = shard_rows // tile_rows
    capacity = -(-(share + tile_rows - 1) // 16) * 16
    i32 = jnp.int32

    onehot = labels[:, None] == jnp.arange(clusters, dtype=i32)[None, :]
    held = jnp.sum(onehot.astype(i32), axis=0)
    every = lax.all_gather(held, ("tr", "tc"), axis=0, tiled=False)
    every = every.reshape(tile_rows, columns, clusters)
    column = lax.dynamic_index_in_dim(every, place, 1, keepdims=False)

    index = jnp.arange(shard_rows, dtype=i32)
    lower = (index[:, None] > index[None, :]).astype(jnp.bfloat16)
    ahead = jnp.dot(lower, onehot.astype(jnp.bfloat16), preferred_element_type=jnp.float32)
    rank = jnp.sum(jnp.where(onehot, ahead, 0.0), axis=1).astype(i32)
    starts = exclusive(held, 0)
    order = jnp.sum(jnp.where(onehot, starts[None, :], 0), axis=1) + rank

    values = embeddings.astype(jnp.float32)
    unit = (values * lax.rsqrt(jnp.sum(values * values, axis=1, keepdims=True) + EPSILON)).astype(
        jnp.bfloat16
    )
    width = feature_dim // CHUNKS
    parts = [unit[:, c * width : (c + 1) * width] for c in range(CHUNKS)]

    def exchange(part, count):
        return lax.all_to_all(
            part.reshape(tile_rows, count, width), "tr", split_axis=0, concat_axis=0, tiled=True
        ).reshape(tile_rows * count, width)

    spread = permute(order % tile_rows * share + order // tile_rows, shard_rows, parts)
    spread = [exchange(part, share) for part in spread]

    local = exclusive(column, 1)
    group_count = column.reshape(tile_rows, tile_rows, GROUP_CLUSTERS).sum(2)
    group_start = exclusive(group_count, 1)
    via = jnp.arange(tile_rows, dtype=i32)

    def before(limit):
        return (limit[..., None] - via + tile_rows - 1) // tile_rows

    first = before(group_start)
    passed = before(group_start + group_count) - first
    base = exclusive(passed, 0) - first

    number = jnp.arange(share, dtype=i32)[None, :] * tile_rows + me
    inside = (number[:, :, None] >= group_start[:, None, :]) & (
        number[:, :, None] < (group_start + group_count)[:, None, :]
    )
    my_base = lax.dynamic_index_in_dim(base, me, 2, keepdims=False)
    lane = my_base[:, None, :] + number[:, :, None] // tile_rows
    target = jnp.sum(jnp.where(inside, via * capacity + lane, 0), axis=2).reshape(-1)
    routed = permute(target, tile_rows * capacity, spread)
    routed = [exchange(part, capacity) for part in routed]

    mine = lax.dynamic_slice_in_dim(column, me * GROUP_CLUSTERS, GROUP_CLUSTERS, 1)
    lengths = mine.T.reshape(-1)
    seg_start = exclusive(lengths, 0)
    seg_local = lax.dynamic_slice_in_dim(local, me * GROUP_CLUSTERS, GROUP_CLUSTERS, 1).T.reshape(-1)
    within = (index[:, None] >= seg_start[None, :]) & (
        index[:, None] < (seg_start + lengths)[None, :]
    )
    number = index + jnp.sum(jnp.where(within, (seg_local - seg_start)[None, :], 0), axis=1)
    route = number % tile_rows
    tables = lax.dynamic_index_in_dim(base, me, 1, keepdims=False)
    tables = jnp.tile(tables, (GROUP_CLUSTERS, 1))
    picked = jnp.sum(jnp.where(within[:, :, None], tables[None], 0), axis=1)
    offset = jnp.sum(jnp.where(route[:, None] == via[None, :], picked, 0), axis=1)
    source = route * capacity + offset + number // tile_rows
    matrix = (
        source[:, None] == jnp.arange(tile_rows * capacity, dtype=i32)[None, :]
    ).astype(jnp.bfloat16)
    queries = [
        jnp.dot(matrix, part, preferred_element_type=jnp.float32).astype(jnp.bfloat16)
        for part in routed
    ]
    keys = [lax.all_gather(part, "tc", axis=0, tiled=True) for part in queries]

    totals = lax.dynamic_slice_in_dim(every.sum(0), me * GROUP_CLUSTERS, GROUP_CLUSTERS, 1)
    ends = jnp.cumsum(totals, axis=1)[:, : GROUP_CLUSTERS - 1]
    key_labels = jnp.sum((index[None, :, None] >= ends[:, None, :]).astype(i32), axis=2)
    query_labels = lax.dynamic_index_in_dim(key_labels, place, 0, keepdims=False)

    best, weighted = cluster_stats(queries, keys, query_labels, key_labels.reshape(-1), place)

    back = lax.all_gather(jnp.stack([best, weighted]), "tr", axis=1, tiled=True)
    shard_before = exclusive(column, 0)
    begin = exclusive(column.sum(0), 0) + lax.dynamic_index_in_dim(
        shard_before, me, 0, keepdims=False
    )
    position = jnp.sum(jnp.where(onehot, begin[None, :], 0), axis=1) + rank
    here = position[:, None] == jnp.arange(tile_rows * shard_rows, dtype=i32)[None, :]
    best_sim = jnp.sum(jnp.where(here, back[0][None, :], 0.0), axis=1)
    mean_sim = jnp.sum(jnp.where(here, back[1][None, :], 0.0), axis=1)
    flag = jax.nn.sigmoid(SHARPNESS * (best_sim - THRESHOLD))
    return (best_sim, mean_sim, flag)


def solution(mesh):
    placed = (P(("tr", "tc"), None), P(("tr", "tc")))
    return jax.shard_map(
        per_device,
        mesh=mesh,
        in_specs=placed,
        out_specs=(P(("tr", "tc")), P(("tr", "tc")), P(("tr", "tc"))),
        check_vma=False,
    )
```

time: 302 us -> 266 us (0.88)
  blocking collectives: 9.12 us -> 107 us
  waiting for transfers between devices: 162 us -> 81.8 us
  local copies, waits for them, and re-layouts: 41.5 us -> 9.52 us
  Pallas kernels: 0 us -> 28.6 us
  other arithmetic: 29.7 us -> 9.92 us
  matrix products: 28 us -> 9.99 us
  starting transfers between devices: 16 us -> 7.17 us
    all_to_all x3 -> x2, waiting for transfers between devices: 109 us -> 38.2 us  [exchange(): lax.all_to_all(part.reshape(tile_rows, count, width), 'tr', split_axis=0,...]
    all_to_all x0 -> x2, blocking collectives: none -> 45.6 us  [exchange(): lax.all_to_all(part.reshape(tile_rows, count, width), 'tr', split_axis=0,...]
    unnamed x0 -> x1, blocking collectives: none -> 42 us
    pallas_call x0 -> x1, Pallas kernels: none -> 28.6 us  [cluster_stats(): pl.pallas_call(functools.partial(stats_kernel, chunks), grid=(members //...]
    scatter x3 -> x0, local copies, waits for them, and re-layouts: 27.6 us -> none  [the longest x1 15.1 us: per_device(): jnp.zeros((shard_rows, feature_dim), jnp.bfloat16).at[target]]
    dot_general x8 -> x7, matrix products: 28 us -> 9.99 us  [the longest x4 5.03 us: permute(): jnp.dot(matrix, part, preferred_element_type=jnp.float32)]
    all_gather x1, blocking collectives: 9.12 us -> 19.2 us  [per_device(): back = lax.all_gather(jnp.stack([best, weighted]), 'tr', axis=1, tiled=True)]
    all_gather x1 -> x2, waiting for transfers between devices: 53.2 us -> 43.5 us  [per_device(): keys = [lax.all_gather(part, 'tc', axis=0, tiled=True) for part in queries]]
  transfers between devices with their start and end apart: 4 -> 4, of which waited for: 3 -> 3; matrix products, arithmetic and copies ran while one was open for 7% -> 2% of each run, Pallas kernels for 0% -> 0%
where the time goes in v1:
time: 266 us; the launch traced here: 268 us
  blocking collectives  107 us (40%)
  waiting for transfers between devices  81.8 us (31%)
  Pallas kernels  28.6 us (11%)
  between operations  14.3 us (5%)
  matrix products  9.99 us (4%)
  other arithmetic  9.92 us (4%)
  local copies, waits for them, and re-layouts  9.52 us (4%)
  starting transfers between devices  7.17 us (3%)
    all_to_all x2, blocking collectives, exchange(): lax.all_to_all(part.reshape(tile_rows, count, width), 'tr', split_axis=0,...  45.6 us
    all_gather x2, waiting for transfers between devices, per_device(): keys = [lax.all_gather(part, 'tc', axis=0, tiled=True) for part in queries]  43.5 us
    unnamed x1, blocking collectives  42 us
    all_to_all x2, waiting for transfers between devices, exchange(): lax.all_to_all(part.reshape(tile_rows, count, width), 'tr', split_axis=0,...  38.2 us
    pallas_call x1, Pallas kernels, cluster_stats(): pl.pallas_call(functools.partial(stats_kernel, chunks), grid=(members //...  28.6 us
    all_gather x1, blocking collectives, per_device(): back = lax.all_gather(jnp.stack([best, weighted]), 'tr', axis=1, tiled=True)  19.2 us
    unnamed x18, local copies, waits for them, and re-layouts  7.13 us
    all_to_all x2, starting transfers between devices, exchange(): lax.all_to_all(part.reshape(tile_rows, count, width), 'tr', split_axis=0,...  7.09 us
  transfers between devices with their start and end apart: 4, of which 3 were waited for; matrix products, arithmetic and copies ran while one was open for 2% of the time, Pallas kernels for 0%

profile of v1, /device:TPU:0, one launch (start us, length us, event | category | flops | bytes accessed | tf_op | source)
XLA Modules:
  0.0 268.1 jit_solution(2146407809479377066)
XLA Ops:
  7.2 0.9 convert_reduce_fusion.1
  8.1 1.1 fusion.22
  9.5 42.0 %all-reduce = s32[512]{0:T(512)S(1)} all-reduce(s32[512]{0:T(512)S(1)} %dynamic-update-slice), channel_id=2, replica_groups=mesh['tr'=4,'tc'=8] {'tr','tc'}, use_global_device_ids=true, to_apply=%add | all-reduce | flops 512 | bytes 4096
  52.1 0.7 fusion.48
  53.0 1.8 fusion
  55.7 1.7 fusion.13
  57.4 3.6 %all-to-all-start = ((bf16[4,192,512]{2,1,0:T(8,128)(2,1)}), bf16[4,192,512]{2,1,0:T(8,128)(2,1)S(1)}, u32[]{:S(2)}, u32[]{:S(2)}) async-start(bf16[4,192,512]{2,1,0:T(8,128)(2,1)} %bitcast.15), calls=%async_computation | async-start | bytes 1572864 | tf_op jit(solution)/shard_map/all_to_all | solution.py:177
  61.9 18.5 %all-to-all-done = bf16[4,192,512]{2,1,0:T(8,128)(2,1)S(1)} async-done(((bf16[4,192,512]{2,1,0:T(8,128)(2,1)}), bf16[4,192,512]{2,1,0:T(8,128)(2,1)S(1)}, u32[]{:S(2)}, u32[]{:S(2)}) %all-to-all-start) | async-done | bytes 786464 | tf_op jit(solution)/shard_map/all_to_all | solution.py:177
  80.4 1.7 fusion.9
  82.2 3.5 %all-to-all-start.1 = ((bf16[4,208,512]{2,1,0:T(8,128)(2,1)}), bf16[4,208,512]{2,1,0:T(8,128)(2,1)S(1)}, u32[]{:S(2)}, u32[]{:S(2)}) async-start(bf16[4,208,512]{2,1,0:T(8,128)(2,1)} %bitcast.17), calls=%async_computation.1 | async-start | bytes 1703936 | tf_op jit(solution)/shard_map/all_to_all | solution.py:177
  86.9 19.7 %all-to-all-done.1 = bf16[4,208,512]{2,1,0:T(8,128)(2,1)S(1)} async-done(((bf16[4,208,512]{2,1,0:T(8,128)(2,1)}), bf16[4,208,512]{2,1,0:T(8,128)(2,1)S(1)}, u32[]{:S(2)}, u32[]{:S(2)}) %all-to-all-start.1) | async-done | bytes 852000 | tf_op jit(solution)/shard_map/all_to_all | solution.py:177
  106.6 2.0 fusion.11.refs_0_
  108.7 0.8 fusion.14
  109.4 22.1 %all_to_all.20 = bf16[4,192,512]{2,1,0:T(8,128)(2,1)S(1)} all-to-all(bf16[4,192,512]{2,1,0:T(8,128)(2,1)S(1)} %bitcast.43), channel_id=1, replica_groups=mesh['tr'=4,'tc'=8] {'tr'}, dimensions={0} | all-to-all | bytes 1572864 | tf_op jit(solution)/shard_map/all_to_all | solution.py:177
  131.5 0.8 fusion.10
  132.3 23.5 %all_to_all.21 = bf16[4,208,512]{2,1,0:T(8,128)(2,1)S(1)} all-to-all(bf16[4,208,512]{2,1,0:T(8,128)(2,1)S(1)} %bitcast.40), channel_id=1, replica_groups=mesh['tr'=4,'tc'=8] {'tr'}, dimensions={0} | all-to-all | bytes 1703936 | tf_op jit(solution)/shard_map/all_to_all | solution.py:177
  155.9 1.9 fusion.12.refs_1_
  158.9 43.5 %all-gather.6.cloned.1.call-done.refs_3_ = bf16[6144,512]{1,0:T(8,128)(2,1)} async-done(((bf16[768,512]{1,0:T(8,128)(2,1)}), bf16[6144,512]{1,0:T(8,128)(2,1)}) %all-gather.6.cloned.1.call-update) | async-done | bytes 6291472 | tf_op jit(solution)/shard_map/all_gather | solution.py:227
  202.4 1.1 copy-done.1
  203.5 2.8 %copy-done.2 = bf16[6144,512]{1,0:T(8,128)(2,1)S(1)} copy-done((bf16[6144,512]{1,0:T(8,128)(2,1)S(1)}, bf16[6144,512]{1,0:T(8,128)(2,1)}, u32[]{:S(2)}) %copy-start.2) | copy-done | bytes 6291480
  206.3 2.8 %copy-done.3 = bf16[6144,512]{1,0:T(8,128)(2,1)S(1)} copy-done((bf16[6144,512]{1,0:T(8,128)(2,1)S(1)}, bf16[6144,512]{1,0:T(8,128)(2,1)}, u32[]{:S(2)}) %copy-start.3) | copy-done | bytes 6291480
  209.1 28.6 %shard_map.49 = (f32[768,1]{1,0:T(8,128)S(1)}, f32[768,1]{1,0:T(8,128)S(1)}) custom-call(s32[3]{0:T(128)S(1)} %get-tuple-element.12.q_lo, s32[3]{0:T(128)S(1)} %get-tuple-element.11.q_hi, s32[24]{0:T(128)S(1)} %bitcast.38, s32[24]{0:T(128)S(1)} %bitcast.37, s32[1]{0:T(128)} %bitcast.5.place, s32[768,1]{1,0:T(8,128)S(1)} %copy.60.q_labels, ...), custom_call_target="tpu_custom_call" | custom-call | flops 9663676416 | bytes 12582912 | tf_op jit(solution)/shard_map/pallas_call | solution.py:97
  238.1 19.2 %all_gather.19 = f32[2,3072]{1,0:T(2,128)S(1)} all-gather(f32[2,768]{1,0:T(2,128)S(1)} %pad_maximum_fusion), channel_id=1, replica_groups=mesh['tr'=4,'tc'=8] {'tr'}, dimensions={1}, use_global_device_ids=true | all-gather | bytes 30720 | tf_op jit(solution)/shard_map/all_gather | solution.py:236
  257.4 3.3 %select_reduce_fusion = (f32[768]{0:T(1024)}, f32[768]{0:T(1024)S(1)}) fusion(f32[3072]{0:T(1024)S(1)} %bitcast.50, s32[768]{0:T(1024)S(1)} %get-tuple-element.24, f32[3072]{0:T(1024)S(1)} %bitcast.49), kind=kLoop, calls=%fused_computation | loop fusion | flops 11794944 | bytes 33792 | tf_op jit(solution)/shard_map/reduce_sum | solution.py:244
  (86 shorter events, 6.2 us)
Async XLA Ops:
  7.2 48.1 %copy-start.4 = (bf16[768,1024]{1,0:T(8,128)(2,1)S(1)}, bf16[768,1024]{1,0:T(8,128)(2,1)}, u32[]{:S(2)}) copy-start(bf16[768,1024]{1,0:T(8,128)(2,1)} %param.2) | copy-start | bytes 4718596
  9.2 46.4 %copy-start.5 = (s32[768]{0:T(1024)S(1)}, s32[768]{0:T(1024)}, u32[]{:S(2)}) copy-start(s32[768]{0:T(1024)} %param.3) | copy-start | bytes 9220
  57.4 23.0 %all-to-all-start = ((bf16[4,192,512]{2,1,0:T(8,128)(2,1)}), bf16[4,192,512]{2,1,0:T(8,128)(2,1)S(1)}, u32[]{:S(2)}, u32[]{:S(2)}) async-start(bf16[4,192,512]{2,1,0:T(8,128)(2,1)} %bitcast.15), calls=%async_computation | async-start | bytes 1572864 | tf_op jit(solution)/shard_map/all_to_all | solution.py:177
  82.2 24.5 %all-to-all-start.1 = ((bf16[4,208,512]{2,1,0:T(8,128)(2,1)}), bf16[4,208,512]{2,1,0:T(8,128)(2,1)S(1)}, u32[]{:S(2)}, u32[]{:S(2)}) async-start(bf16[4,208,512]{2,1,0:T(8,128)(2,1)} %bitcast.17), calls=%async_computation.1 | async-start | bytes 1703936 | tf_op jit(solution)/shard_map/all_to_all | solution.py:177
  85.7 73.2 %all-gather.4.cloned.1.call-start = ((), (), s32[]{:S(2)}) async-start(), calls=%async_computation.4 | async-start | bytes 7077888 | tf_op jit(solution)/shard_map/all_gather | solution.py:227
  108.6 93.8 %all-gather.6.cloned.1.call-start = ((), (), s32[]{:S(2)}) async-start(), calls=%async_computation.5 | async-start | bytes 7077888 | tf_op jit(solution)/shard_map/all_gather | solution.py:227
  155.9 46.6 %copy-start = (bf16[768,512]{1,0:T(8,128)(2,1)S(1)}, bf16[768,512]{1,0:T(8,128)(2,1)}, u32[]{:S(2)}) copy-start(bf16[768,512]{1,0:T(8,128)(2,1)} %fusion.11.refs_0_) | copy-start | bytes 2359300
  202.4 1.1 copy-start.1
  203.5 2.8 %copy-start.2 = (bf16[6144,512]{1,0:T(8,128)(2,1)S(1)}, bf16[6144,512]{1,0:T(8,128)(2,1)}, u32[]{:S(2)}) copy-start(bf16[6144,512]{1,0:T(8,128)(2,1)} %all-gather.4.cloned.1.call-done.refs_2_) | copy-start | bytes 18874372
  206.3 2.8 %copy-start.3 = (bf16[6144,512]{1,0:T(8,128)(2,1)S(1)}, bf16[6144,512]{1,0:T(8,128)(2,1)}, u32[]{:S(2)}) copy-start(bf16[6144,512]{1,0:T(8,128)(2,1)} %all-gather.6.cloned.1.call-done.refs_3_) | copy-start | bytes 18874372
  260.7 0.6 copy-start.6
Sparse Core Ops, SparseCore 0:
  108.7 44.4 all-gather.3
  157.9 44.4 all-gather.5

commit v2 on v1

--- a/solution.py
+++ b/solution.py
@@ -16,7 +16,8 @@
 THRESHOLD = 0.3
 SHARPNESS = 50.0
 TILE = 256
-CHUNKS = 2
+CHUNKS = 1
+MESH = pl.DeviceIdType.MESH
 
 
 def stats_kernel(chunks, q_lo, q_hi, k_lo, k_hi, place, q_labels, k_labels, *refs):
@@ -130,6 +131,216 @@
     return best[:, 0], weighted[:, 0]
 
 
+def count_kernel(rows, columns, held, column, totals, mine, sems):
+    me, place = lax.axis_index("tr"), lax.axis_index("tc")
+    tr_peers = [lax.rem(me + d, rows) for d in range(1, rows)]
+    tc_peers = [lax.rem(place + d, columns) for d in range(1, columns)]
+    barrier = pltpu.get_barrier_semaphore()
+    for peer in tr_peers:
+        pl.semaphore_signal(barrier, inc=1, device_id=(peer, place), device_id_type=MESH)
+    for peer in tc_peers:
+        pl.semaphore_signal(barrier, inc=1, device_id=(me, peer), device_id_type=MESH)
+    pl.semaphore_wait(barrier, rows + columns - 2)
+
+    def exchange(source, buffer, index, peers, first, whom):
+        copies = []
+        for d, peer in enumerate(peers):
+            copy = pltpu.make_async_remote_copy(
+                src_ref=source,
+                dst_ref=buffer.at[index],
+                send_sem=sems.at[0, first + d],
+                recv_sem=sems.at[1, first + d],
+                device_id=whom(peer),
+                device_id_type=MESH,
+            )
+            copy.start()
+            copies.append(copy)
+        buffer[index] = source[...]
+        for copy in copies:
+            copy.wait()
+
+    exchange(held, column, me, tr_peers, 0, lambda peer: (peer, place))
+    mine[...] = jnp.sum(column[...], axis=0)
+    exchange(mine, totals, place, tc_peers, rows - 1, lambda peer: (me, peer))
+
+
+def gather_counts(held, rows, columns):
+    clusters = held.shape[0]
+    padded = jnp.zeros((8, 128), jnp.int32).at[0, :clusters].set(held)
+    vmem = pl.BlockSpec(memory_space=pltpu.VMEM)
+    column, totals = pl.pallas_call(
+        functools.partial(count_kernel, rows, columns),
+        in_specs=[vmem],
+        out_specs=[vmem, vmem],
+        out_shape=[
+            jax.ShapeDtypeStruct((rows, 8, 128), jnp.int32),
+            jax.ShapeDtypeStruct((columns, 8, 128), jnp.int32),
+        ],
+        scratch_shapes=[
+            pltpu.VMEM((8, 128), jnp.int32),
+            pltpu.SemaphoreType.DMA((2, rows + columns - 2)),
+        ],
+        compiler_params=pltpu.CompilerParams(collective_id=0, has_side_effects=True),
+    )(padded)
+    return column[:, 0, :clusters], totals[:, 0, :clusters]
+
+
+def plane_kernel(tile_rows, q_labels, k_labels, own, back, blocks, stats, part, theirs, sems):
+    me, place = lax.axis_index("tr"), lax.axis_index("tc")
+    sibling = place + 1 - 2 * (place % 2)
+    across = place + 2 - 4 * ((place // 2) % 2)
+    along = place + 4 - 8 * (place // 4)
+    rows = own.shape[0]
+    tiles = rows // TILE
+    peers = [(me, sibling), (me, across), (me, along)]
+    peers += [(lax.rem(me + d, tile_rows), place) for d in range(1, tile_rows)]
+    barrier = pltpu.get_barrier_semaphore()
+    for peer in peers:
+        pl.semaphore_signal(barrier, inc=1, device_id=peer, device_id_type=MESH)
+    pl.semaphore_wait(barrier, len(peers))
+
+    def send(source, target, number, peer):
+        copy = pltpu.make_async_remote_copy(
+            src_ref=source,
+            dst_ref=target,
+            send_sem=sems.at[0, number],
+            recv_sem=sems.at[1, number],
+            device_id=peer,
+            device_id_type=MESH,
+        )
+        copy.start()
+        return copy
+
+    def cut(c):
+        return pl.ds(c * TILE, TILE)
+
+    direct, passed = [], []
+    for c in range(tiles):
+        direct.append(
+            [
+                send(own.at[cut(c), :], blocks.at[2, cut(c), :], 4 * c, peers[1]),
+                send(own.at[cut(c), :], blocks.at[3, cut(c), :], 4 * c + 1, peers[2]),
+            ]
+        )
+    from_sibling = send(own, blocks.at[1], 4 * tiles, peers[0])
+    blocks[0] = own[...]
+    for side in range(2):
+        stats[side, 0] = jnp.full((rows, 128), NEGATIVE, jnp.float32)
+        stats[side, 1] = jnp.zeros((rows, 128), jnp.float32)
+        stats[side, 2] = jnp.zeros((rows, 128), jnp.float32)
+
+    def tile(side, qt, ks, kc, itself=False):
+        q_rows = pl.ds(pl.multiple_of(qt * TILE, TILE), TILE)
+        k_rows = pl.ds(pl.multiple_of(kc * TILE, TILE), TILE)
+        sims = lax.dot_general(
+            blocks[2 * side, q_rows, :],
+            blocks[ks, k_rows, :],
+            (((1,), (1,)), ((), ())),
+            preferred_element_type=jnp.float32,
+        )
+        mask = q_labels[side, q_rows, :] == k_labels[ks, kc]
+        if itself:
+            row = lax.broadcasted_iota(jnp.int32, (TILE, TILE), 0) + qt * TILE
+            col = lax.broadcasted_iota(jnp.int32, (TILE, TILE), 1) + kc * TILE
+            mask = mask & (row != col)
+        sims = jnp.where(mask, sims, NEGATIVE)
+        left, right = sims[:, :128], sims[:, 128:]
+        old = stats[side, 0, q_rows, :]
+        top = jnp.maximum(old, jnp.maximum(left, right))
+        factor = jnp.exp(SCALE * (old - top))
+        left_term = jnp.exp(SCALE * (left - top))
+        right_term = jnp.exp(SCALE * (right - top))
+        stats[side, 0, q_rows, :] = top
+        stats[side, 1, q_rows, :] = stats[side, 1, q_rows, :] * factor + (left_term + right_term)
+        stats[side, 2, q_rows, :] = stats[side, 2, q_rows, :] * factor + (
+            left_term * left + right_term * right
+        )
+
+    def each(count, body):
+        lax.fori_loop(0, count, lambda i, none: (body(i), none)[1], 0)
+
+    each(tiles * tiles, lambda i: tile(0, i // tiles, 0, i % tiles, itself=True))
+    from_sibling.wait()
+    each(tiles * tiles, lambda i: tile(0, i // tiles, 1, i % tiles))
+    for c in range(tiles):
+        for axis in range(2):
+            direct[c][axis].wait()
+            passed.append(
+                send(
+                    blocks.at[2 + axis, cut(c), :],
+                    blocks.at[4 + axis, cut(c), :],
+                    4 * c + 2 + axis,
+                    peers[0],
+                )
+            )
+        each(2 * tiles, lambda i: tile(0, i // 2, 2 + i % 2, c))
+        each(c + 1, lambda i: tile(1, i, 3, c))
+        if c:
+            each(c, lambda i: tile(1, c, 3, i))
+        passed[2 * c].wait()
+        passed[2 * c + 1].wait()
+        each(c + 1, lambda i: tile(1, i, 5, c))
+        if c:
+            each(c, lambda i: tile(1, c, 5, i))
+        if c < tiles - 1:
+            each(2 * tiles, lambda i: tile(0, i // 2, 4 + i % 2, c))
+
+    def fold(side):
+        top = stats[side, 0]
+        best = jnp.max(top, axis=1, keepdims=True)
+        factor = jnp.exp(SCALE * (top - best))
+        total = jnp.sum(stats[side, 1] * factor, axis=1, keepdims=True)
+        weight = jnp.sum(stats[side, 2] * factor, axis=1, keepdims=True)
+        lane = lax.broadcasted_iota(jnp.int32, (rows, 128), 1)
+        packed = jnp.where(lane == 0, best, jnp.where(lane == 1, total, weight))
+        return packed.T[:8]
+
+    part[1] = fold(1)
+    diagonal = send(part.at[1], theirs, 4 * tiles + 1, peers[1])
+    each(2 * tiles, lambda i: tile(0, i // 2, 4 + i % 2, tiles - 1))
+    mine = fold(0)
+    diagonal.wait()
+    other = theirs[...]
+    best = jnp.maximum(mine[0:1], other[0:1])
+    ours, others = jnp.exp(SCALE * (mine[0:1] - best)), jnp.exp(SCALE * (other[0:1] - best))
+    total = mine[1:2] * ours + other[1:2] * others
+    weight = mine[2:3] * ours + other[2:3] * others
+    line = lax.broadcasted_iota(jnp.int32, (8, rows), 0)
+    part[0] = jnp.where(line == 0, best, weight / total)
+    home = [
+        send(part.at[0], back.at[me], 4 * tiles + 1 + d, peers[2 + d]) for d in range(1, tile_rows)
+    ]
+    back[me] = part[0]
+    for copy in home:
+        copy.wait()
+
+
+def plane_stats(queries, key_labels, place, tile_rows):
+    rows, width = queries.shape
+    tiles = rows // TILE
+    order = [0, 1, 2, 4, 3, 5]
+    near = jnp.stack(
+        [lax.dynamic_index_in_dim(key_labels, place ^ n, 0, keepdims=False) for n in order]
+    )
+    vmem = pl.BlockSpec(memory_space=pltpu.VMEM)
+    return pl.pallas_call(
+        functools.partial(plane_kernel, tile_rows),
+        in_specs=[vmem] * 3,
+        out_specs=vmem,
+        out_shape=jax.ShapeDtypeStruct((tile_rows, 8, rows), jnp.float32),
+        scratch_shapes=[
+            pltpu.VMEM((6, rows, width), jnp.bfloat16),
+            pltpu.VMEM((2, 3, rows, 128), jnp.float32),
+            pltpu.VMEM((2, 8, rows), jnp.float32),
+            pltpu.VMEM((8, rows), jnp.float32),
+            pltpu.SemaphoreType.DMA((2, 4 * tiles + 1 + tile_rows)),
+        ],
+        compiler_params=pltpu.CompilerParams(
+            collective_id=1, has_side_effects=True, vmem_limit_bytes=40 << 20
+        ),
+    )(near[jnp.array([0, 2])][:, :, None], near.reshape(6, tiles, 1, TILE), queries)
+
+
 def permute(target, count, parts):
     matrix = (jnp.arange(count, dtype=jnp.int32)[:, None] == target[None, :]).astype(jnp.bfloat16)
     return [
@@ -155,9 +366,7 @@
 
     onehot = labels[:, None] == jnp.arange(clusters, dtype=i32)[None, :]
     held = jnp.sum(onehot.astype(i32), axis=0)
-    every = lax.all_gather(held, ("tr", "tc"), axis=0, tiled=False)
-    every = every.reshape(tile_rows, columns, clusters)
-    column = lax.dynamic_index_in_dim(every, place, 1, keepdims=False)
+    column, everywhere = gather_counts(held, tile_rows, columns)
 
     index = jnp.arange(shard_rows, dtype=i32)
     lower = (index[:, None] > index[None, :]).astype(jnp.bfloat16)
@@ -224,16 +433,18 @@
         jnp.dot(matrix, part, preferred_element_type=jnp.float32).astype(jnp.bfloat16)
         for part in routed
     ]
-    keys = [lax.all_gather(part, "tc", axis=0, tiled=True) for part in queries]
-
-    totals = lax.dynamic_slice_in_dim(every.sum(0), me * GROUP_CLUSTERS, GROUP_CLUSTERS, 1)
+    totals = lax.dynamic_slice_in_dim(everywhere, me * GROUP_CLUSTERS, GROUP_CLUSTERS, 1)
     ends = jnp.cumsum(totals, axis=1)[:, : GROUP_CLUSTERS - 1]
     key_labels = jnp.sum((index[None, :, None] >= ends[:, None, :]).astype(i32), axis=2)
-    query_labels = lax.dynamic_index_in_dim(key_labels, place, 0, keepdims=False)
-
-    best, weighted = cluster_stats(queries, keys, query_labels, key_labels.reshape(-1), place)
-
-    back = lax.all_gather(jnp.stack([best, weighted]), "tr", axis=1, tiled=True)
+
+    if columns == 8:
+        back = plane_stats(queries[0], key_labels, place, tile_rows)
+        back = jnp.stack([back[:, 0].reshape(-1), back[:, 1].reshape(-1)])
+    else:
+        keys = [lax.all_gather(part, "tc", axis=0, tiled=True) for part in queries]
+        query_labels = lax.dynamic_index_in_dim(key_labels, place, 0, keepdims=False)
+        best, weighted = cluster_stats(queries, keys, query_labels, key_labels.reshape(-1), place)
+        back = lax.all_gather(jnp.stack([best, weighted]), "tr", axis=1, tiled=True)
     shard_before = exclusive(column, 0)
     begin = exclusive(column.sum(0), 0) + lax.dynamic_index_in_dim(
         shard_before, me, 0, keepdims=False

time: 266 us -> 167 us (0.63)
  blocking collectives: 107 us -> 0 us
  Pallas kernels: 28.6 us -> 63.3 us
  between operations: 14.3 us -> 0.89 us
  waiting for transfers between devices: 81.8 us -> 73 us
  local copies, waits for them, and re-layouts: 9.52 us -> 3.62 us
    all_to_all x2 -> x0, blocking collectives: 45.6 us -> none  [exchange(): lax.all_to_all(part.reshape(tile_rows, count, width), 'tr', split_axis=0,...]
    all_gather x2 -> x0, waiting for transfers between devices: 43.5 us -> none  [per_device(): keys = [lax.all_gather(part, 'tc', axis=0, tiled=True) for part in queries]]
    unnamed x1 -> x0, blocking collectives: 42 us -> none
    all_to_all x2, waiting for transfers between devices: 38.2 us -> 73 us  [exchange(): lax.all_to_all(part.reshape(tile_rows, count, width), 'tr', split_axis=0,...]
    pallas_call x1 -> x2, Pallas kernels: 28.6 us -> 63.3 us  [the longest x1 50.5 us: plane_stats(): pl.pallas_call(functools.partial(plane_kernel, tile_rows), in_specs=[vmem...]
    all_gather x1 -> x0, blocking collectives: 19.2 us -> none  [per_device(): back = lax.all_gather(jnp.stack([best, weighted]), 'tr', axis=1, tiled=True)]
    unnamed x18 -> x6, local copies, waits for them, and re-layouts: 7.13 us -> 0.02 us
    dot_general x4 -> x2, matrix products: 5.03 us -> 5.32 us  [permute(): jnp.dot(matrix, part, preferred_element_type=jnp.float32)]
  transfers between devices with their start and end apart: 4 -> 2, of which waited for: 3 -> 2; matrix products, arithmetic and copies ran while one was open for 2% -> 2% of each run, Pallas kernels for 0% -> 0%
where the time goes in v2:
time: 167 us
  waiting for transfers between devices  73 us (44%)
  Pallas kernels  63.3 us (38%)
  other arithmetic  9.19 us (6%)
  starting transfers between devices  8.27 us (5%)
  matrix products  8.26 us (5%)
  local copies, waits for them, and re-layouts  3.62 us (2%)
    all_to_all x2, waiting for transfers between devices, exchange(): lax.all_to_all(part.reshape(tile_rows, count, width), 'tr', split_axis=0,...  73 us
    pallas_call x1, Pallas kernels, plane_stats(): pl.pallas_call(functools.partial(plane_kernel, tile_rows), in_specs=[vmem...  50.5 us
    pallas_call x1, Pallas kernels, gather_counts(): pl.pallas_call(functools.partial(count_kernel, rows, columns), in_specs=[...  12.8 us
    all_to_all x2, starting transfers between devices, exchange(): lax.all_to_all(part.reshape(tile_rows, count, width), 'tr', split_axis=0,...  8.27 us
    dot_general x2, matrix products, permute(): jnp.dot(matrix, part, preferred_element_type=jnp.float32)  5.32 us
  transfers between devices with their start and end apart: 2, of which 2 were waited for; matrix products, arithmetic and copies ran while one was open for 2% of the time, Pallas kernels for 0%

profile of v2, /device:TPU:0, one launch (start us, length us, event | category | flops | bytes accessed | tf_op | source)
XLA Modules:
  0.0 166.5 jit_solution(8003414499883610054)
XLA Ops:
  0.7 0.9 convert_reduce_fusion.1
  1.6 0.6 scatter.4.held
  2.2 12.8 %shard_map.58 = (s32[4,8,128]{2,1,0:T(8,128)}, s32[8,8,128]{2,1,0:T(8,128)}) custom-call(s32[8,128]{1,0:T(8,128)} %scatter.4.held), custom_call_target="tpu_custom_call" | custom-call | tf_op jit(solution)/shard_map/pallas_call | solution.py:171
  15.0 0.7 slice_reduce_fusion.1
  15.8 0.2 reduce_window_sum.68
  16.3 1.1 fusion.15
  17.8 0.2 reduce-window_clone.1
  18.2 0.1 reduce.5
  18.3 1.8 %fusion = f32[768]{0:T(1024)S(1)} fusion(bf16[768,1024]{1,0:T(8,128)(2,1)} %param.5), kind=kLoop, calls=%fused_computation.6 | loop fusion | flops 2358528 | bytes 1575936 | tf_op jit(solution)/shard_map/reduce_sum | solution.py:379
  20.3 2.6 %fusion.7 = bf16[768,1024]{1,0:T(8,128)(2,1)} fusion(bf16[768,1024]{1,0:T(8,128)(2,1)S(1)} %copy-done, f32[768]{0:T(1024)S(1)} %add_rsqrt_fusion, s32[768]{0:T(1024)S(1)} %get-tuple-element.37), kind=kOutput, calls=%fused_computation.17 | convolution fusion | flops 1211695104 | bytes 3151872 | tf_op jit(solution)/shard_map/dot_general | solution.py:347
  23.0 4.5 %all-to-all-start = ((bf16[4,192,1024]{2,1,0:T(8,128)(2,1)}), bf16[4,192,1024]{2,1,0:T(8,128)(2,1)S(1)}, u32[]{:S(2)}, u32[]{:S(2)}) async-start(bf16[4,192,1024]{2,1,0:T(8,128)(2,1)} %bitcast.14), calls=%async_computation | async-start | bytes 3145728 | tf_op jit(solution)/shard_map/all_to_all | solution.py:386
  27.6 0.1 reduce_sum.132
  27.7 0.2 reduce_window_sum.69
  28.3 36.5 %all-to-all-done = bf16[4,192,1024]{2,1,0:T(8,128)(2,1)S(1)} async-done(((bf16[4,192,1024]{2,1,0:T(8,128)(2,1)}), bf16[4,192,1024]{2,1,0:T(8,128)(2,1)S(1)}, u32[]{:S(2)}, u32[]{:S(2)}) %all-to-all-start) | async-done | bytes 1572896 | tf_op jit(solution)/shard_map/all_to_all | solution.py:386
  64.7 2.7 %fusion.6 = bf16[832,1024]{1,0:T(8,128)(2,1)} fusion(bf16[768,1024]{1,0:T(8,128)(2,1)S(1)} %bitcast.30, s32[768]{0:T(1024)S(1)} %eq.94), kind=kOutput, calls=%fused_computation.16 | convolution fusion | flops 1310113792 | bytes 3279872 | tf_op jit(solution)/shard_map/dot_general | solution.py:347
  67.4 3.8 %all-to-all-start.1 = ((bf16[4,208,1024]{2,1,0:T(8,128)(2,1)}), bf16[4,208,1024]{2,1,0:T(8,128)(2,1)S(1)}, u32[]{:S(2)}, u32[]{:S(2)}) async-start(bf16[4,208,1024]{2,1,0:T(8,128)(2,1)} %bitcast.16), calls=%async_computation.1 | async-start | bytes 3407872 | tf_op jit(solution)/shard_map/all_to_all | solution.py:386
  71.5 0.8 slice.32
  72.7 0.6 gather_fusion
  73.2 0.3 copy.37.q_labels
  73.8 36.5 %all-to-all-done.1 = bf16[4,208,1024]{2,1,0:T(8,128)(2,1)S(1)} async-done(((bf16[4,208,1024]{2,1,0:T(8,128)(2,1)}), bf16[4,208,1024]{2,1,0:T(8,128)(2,1)S(1)}, u32[]{:S(2)}, u32[]{:S(2)}) %all-to-all-start.1) | async-done | bytes 1703968 | tf_op jit(solution)/shard_map/all_to_all | solution.py:386
  110.3 1.8 %fusion.8.own = bf16[768,1024]{1,0:T(8,128)(2,1)S(1)} fusion(bf16[832,1024]{1,0:T(8,128)(2,1)S(1)} %bitcast.29, s32[768]{0:T(1024)S(1)} %fusion.25), kind=kOutput, calls=%fused_computation.18 | convolution fusion | flops 1310048256 | bytes 3279872 | tf_op jit(solution)/shard_map/dot_general | solution.py:433
  112.1 50.5 %shard_map.59 = f32[4,8,768]{2,1,0:T(8,128)S(1)} custom-call(s32[2,768,1]{2,1,0:T(8,128)S(1)} %copy.37.q_labels, s32[6,3,1,256]{3,2,1,0:T(1,128)S(1)} %reshape.365.k_labels, bf16[768,1024]{1,0:T(8,128)(2,1)S(1)} %fusion.8.own), custom_call_target="tpu_custom_call" | custom-call | tf_op jit(solution)/shard_map/pallas_call | solution.py:326
  162.6 3.3 %select_reduce_fusion = (f32[768]{0:T(1024)}, f32[768]{0:T(1024)S(1)}) fusion(f32[3072]{0:T(1024)S(1)} %bitcast.36, s32[768]{0:T(1024)S(1)} %get-tuple-element.36, f32[3072]{0:T(1024)S(1)} %bitcast.35), kind=kLoop, calls=%fused_computation.1 | loop fusion | flops 11794944 | bytes 33792 | tf_op jit(solution)/shard_map/reduce_sum | solution.py:455
  165.9 0.6 add_divide_fusion
  (54 shorter events, 2.4 us)
Async XLA Ops:
  0.6 19.6 %copy-start.1 = (s32[768]{0:T(1024)S(1)}, s32[768]{0:T(1024)}, u32[]{:S(2)}) copy-start(s32[768]{0:T(1024)} %param.6) | copy-start | bytes 9220
  0.6 19.7 %copy-start = (bf16[768,1024]{1,0:T(8,128)(2,1)S(1)}, bf16[768,1024]{1,0:T(8,128)(2,1)}, u32[]{:S(2)}) copy-start(bf16[768,1024]{1,0:T(8,128)(2,1)} %param.5) | copy-start | bytes 4718596
  23.0 41.8 %all-to-all-start = ((bf16[4,192,1024]{2,1,0:T(8,128)(2,1)}), bf16[4,192,1024]{2,1,0:T(8,128)(2,1)S(1)}, u32[]{:S(2)}, u32[]{:S(2)}) async-start(bf16[4,192,1024]{2,1,0:T(8,128)(2,1)} %bitcast.14), calls=%async_computation | async-start | bytes 3145728 | tf_op jit(solution)/shard_map/all_to_all | solution.py:386
  67.4 42.9 %all-to-all-start.1 = ((bf16[4,208,1024]{2,1,0:T(8,128)(2,1)}), bf16[4,208,1024]{2,1,0:T(8,128)(2,1)S(1)}, u32[]{:S(2)}, u32[]{:S(2)}) async-start(bf16[4,208,1024]{2,1,0:T(8,128)(2,1)} %bitcast.16), calls=%async_computation.1 | async-start | bytes 3407872 | tf_op jit(solution)/shard_map/all_to_all | solution.py:386
  165.9 0.6 copy-start.2

commit v3 on v2

--- a/solution.py
+++ b/solution.py
@@ -16,7 +16,6 @@
 THRESHOLD = 0.3
 SHARPNESS = 50.0
 TILE = 256
-CHUNKS = 1
 MESH = pl.DeviceIdType.MESH
 
 
@@ -185,21 +184,45 @@
     return column[:, 0, :clusters], totals[:, 0, :clusters]
 
 
-def plane_kernel(tile_rows, q_labels, k_labels, own, back, blocks, stats, part, theirs, sems):
+def plane_kernel(
+    tile_rows,
+    q_labels,
+    k_labels,
+    unit,
+    spread,
+    route,
+    settle,
+    back,
+    sent,
+    landed,
+    routed,
+    arrived,
+    blocks,
+    stats,
+    part,
+    theirs,
+    sems,
+):
     me, place = lax.axis_index("tr"), lax.axis_index("tc")
     sibling = place + 1 - 2 * (place % 2)
     across = place + 2 - 4 * ((place // 2) % 2)
     along = place + 4 - 8 * (place // 4)
-    rows = own.shape[0]
+    rows, width = unit.shape
     tiles = rows // TILE
+    share = rows // tile_rows
+    capacity = routed.shape[0] // tile_rows
+    pieces = width // TILE
     peers = [(me, sibling), (me, across), (me, along)]
-    peers += [(lax.rem(me + d, tile_rows), place) for d in range(1, tile_rows)]
+    others = [lax.rem(me + d, tile_rows) for d in range(1, tile_rows)]
+    peers += [(other, place) for other in others]
     barrier = pltpu.get_barrier_semaphore()
     for peer in peers:
         pl.semaphore_signal(barrier, inc=1, device_id=peer, device_id_type=MESH)
     pl.semaphore_wait(barrier, len(peers))
-
-    def send(source, target, number, peer):
+    counter = iter(range(sems.shape[1]))
+
+    def send(source, target, peer):
+        number = next(counter)
         copy = pltpu.make_async_remote_copy(
             src_ref=source,
             dst_ref=target,
@@ -211,23 +234,60 @@
         copy.start()
         return copy
 
-    def cut(c):
-        return pl.ds(c * TILE, TILE)
-
-    direct, passed = [], []
-    for c in range(tiles):
-        direct.append(
-            [
-                send(own.at[cut(c), :], blocks.at[2, cut(c), :], 4 * c, peers[1]),
-                send(own.at[cut(c), :], blocks.at[3, cut(c), :], 4 * c + 1, peers[2]),
-            ]
-        )
-    from_sibling = send(own, blocks.at[1], 4 * tiles, peers[0])
-    blocks[0] = own[...]
+    def exchange(source, target, count, lanes):
+        def slot(row):
+            return pl.ds(pl.multiple_of(row * count, 16), count)
+
+        copies = [
+            send(source.at[slot(other), lanes], target.at[slot(me), lanes], (other, place))
+            for other in others
+        ]
+        target[slot(me), lanes] = source[slot(me), lanes]
+        return copies
+
+    def move(matrix, source, lanes):
+        return jnp.dot(
+            matrix[...], source[:, lanes], preferred_element_type=jnp.float32
+        ).astype(jnp.bfloat16)
+
+    lanes = [pl.ds(f * TILE, TILE) for f in range(pieces)]
+    first, second, direct, from_sibling, passed = [], [], [], [], []
+    for f in range(pieces):
+        sent[:, lanes[f]] = move(spread, unit, lanes[f])
+        first.append(exchange(sent, landed, share, lanes[f]))
     for side in range(2):
         stats[side, 0] = jnp.full((rows, 128), NEGATIVE, jnp.float32)
         stats[side, 1] = jnp.zeros((rows, 128), jnp.float32)
         stats[side, 2] = jnp.zeros((rows, 128), jnp.float32)
+    for f in range(pieces):
+        for copy in first[f]:
+            copy.wait()
+        routed[:, lanes[f]] = move(route, landed, lanes[f])
+        second.append(exchange(routed, arrived, capacity, lanes[f]))
+
+    def forward(f):
+        for axis in range(2):
+            direct[f][axis].wait()
+            passed.append(
+                send(
+                    blocks.at[2 + axis, :, lanes[f]], blocks.at[4 + axis, :, lanes[f]], peers[0]
+                )
+            )
+
+    for f in range(pieces):
+        for copy in second[f]:
+            copy.wait()
+        blocks[0, :, lanes[f]] = move(settle, arrived, lanes[f])
+        own = blocks.at[0, :, lanes[f]]
+        direct.append(
+            [
+                send(own, blocks.at[2, :, lanes[f]], peers[1]),
+                send(own, blocks.at[3, :, lanes[f]], peers[2]),
+            ]
+        )
+        from_sibling.append(send(own, blocks.at[1, :, lanes[f]], peers[0]))
+        if f:
+            forward(f - 1)
 
     def tile(side, qt, ks, kc, itself=False):
         q_rows = pl.ds(pl.multiple_of(qt * TILE, TILE), TILE)
@@ -259,31 +319,17 @@
     def each(count, body):
         lax.fori_loop(0, count, lambda i, none: (body(i), none)[1], 0)
 
-    each(tiles * tiles, lambda i: tile(0, i // tiles, 0, i % tiles, itself=True))
-    from_sibling.wait()
-    each(tiles * tiles, lambda i: tile(0, i // tiles, 1, i % tiles))
-    for c in range(tiles):
-        for axis in range(2):
-            direct[c][axis].wait()
-            passed.append(
-                send(
-                    blocks.at[2 + axis, cut(c), :],
-                    blocks.at[4 + axis, cut(c), :],
-                    4 * c + 2 + axis,
-                    peers[0],
-                )
-            )
-        each(2 * tiles, lambda i: tile(0, i // 2, 2 + i % 2, c))
-        each(c + 1, lambda i: tile(1, i, 3, c))
-        if c:
-            each(c, lambda i: tile(1, c, 3, i))
-        passed[2 * c].wait()
-        passed[2 * c + 1].wait()
-        each(c + 1, lambda i: tile(1, i, 5, c))
-        if c:
-            each(c, lambda i: tile(1, c, 5, i))
-        if c < tiles - 1:
-            each(2 * tiles, lambda i: tile(0, i // 2, 4 + i % 2, c))
+    square = tiles * tiles
+    each(square, lambda i: tile(0, i // tiles, 0, i % tiles, itself=True))
+    forward(pieces - 1)
+    for copy in from_sibling:
+        copy.wait()
+    each(square, lambda i: tile(0, i // tiles, 1, i % tiles))
+    each(2 * square, lambda i: tile(0, i // 2 % tiles, 2 + i % 2, i // 2 // tiles))
+    each(square, lambda i: tile(1, i // tiles, 3, i % tiles))
+    for copy in passed:
+        copy.wait()
+    each(square, lambda i: tile(1, i // tiles, 5, i % tiles))
 
     def fold(side):
         top = stats[side, 0]
@@ -296,8 +342,8 @@
         return packed.T[:8]
 
     part[1] = fold(1)
-    diagonal = send(part.at[1], theirs, 4 * tiles + 1, peers[1])
-    each(2 * tiles, lambda i: tile(0, i // 2, 4 + i % 2, tiles - 1))
+    diagonal = send(part.at[1], theirs, peers[1])
+    each(2 * square, lambda i: tile(0, i // 2 % tiles, 4 + i % 2, i // 2 // tiles))
     mine = fold(0)
     diagonal.wait()
     other = theirs[...]
@@ -307,17 +353,17 @@
     weight = mine[2:3] * ours + other[2:3] * others
     line = lax.broadcasted_iota(jnp.int32, (8, rows), 0)
     part[0] = jnp.where(line == 0, best, weight / total)
-    home = [
-        send(part.at[0], back.at[me], 4 * tiles + 1 + d, peers[2 + d]) for d in range(1, tile_rows)
-    ]
+    home = [send(part.at[0], back.at[me], peer) for peer in peers[3:]]
     back[me] = part[0]
     for copy in home:
         copy.wait()
 
 
-def plane_stats(queries, key_labels, place, tile_rows):
-    rows, width = queries.shape
+def plane_stats(unit, spread, route, settle, key_labels, place, tile_rows):
+    rows, width = unit.shape
     tiles = rows // TILE
+    padded = route.shape[0]
+    copies = width // TILE * (2 * (tile_rows - 1) + 5) + tile_rows
     order = [0, 1, 2, 4, 3, 5]
     near = jnp.stack(
         [lax.dynamic_index_in_dim(key_labels, place ^ n, 0, keepdims=False) for n in order]
@@ -325,28 +371,39 @@
     vmem = pl.BlockSpec(memory_space=pltpu.VMEM)
     return pl.pallas_call(
         functools.partial(plane_kernel, tile_rows),
-        in_specs=[vmem] * 3,
+        in_specs=[vmem] * 6,
         out_specs=vmem,
         out_shape=jax.ShapeDtypeStruct((tile_rows, 8, rows), jnp.float32),
         scratch_shapes=[
+            pltpu.VMEM((rows, width), jnp.bfloat16),
+            pltpu.VMEM((rows, width), jnp.bfloat16),
+            pltpu.VMEM((padded, width), jnp.bfloat16),
+            pltpu.VMEM((padded, width), jnp.bfloat16),
             pltpu.VMEM((6, rows, width), jnp.bfloat16),
             pltpu.VMEM((2, 3, rows, 128), jnp.float32),
             pltpu.VMEM((2, 8, rows), jnp.float32),
             pltpu.VMEM((8, rows), jnp.float32),
-            pltpu.SemaphoreType.DMA((2, 4 * tiles + 1 + tile_rows)),
+            pltpu.SemaphoreType.DMA((2, copies)),
         ],
         compiler_params=pltpu.CompilerParams(
-            collective_id=1, has_side_effects=True, vmem_limit_bytes=40 << 20
+            collective_id=1, has_side_effects=True, vmem_limit_bytes=48 << 20
         ),
-    )(near[jnp.array([0, 2])][:, :, None], near.reshape(6, tiles, 1, TILE), queries)
-
-
-def permute(target, count, parts):
-    matrix = (jnp.arange(count, dtype=jnp.int32)[:, None] == target[None, :]).astype(jnp.bfloat16)
-    return [
-        jnp.dot(matrix, part, preferred_element_type=jnp.float32).astype(jnp.bfloat16)
-        for part in parts
-    ]
+    )(
+        near[jnp.array([0, 2])][:, :, None],
+        near.reshape(6, tiles, 1, TILE),
+        unit,
+        spread,
+        route,
+        settle,
+    )
+
+
+def placing(target, count):
+    return (jnp.arange(count, dtype=jnp.int32)[:, None] == target[None, :]).astype(jnp.bfloat16)
+
+
+def permute(matrix, part):
+    return jnp.dot(matrix, part, preferred_element_type=jnp.float32).astype(jnp.bfloat16)
 
 
 def exclusive(values, axis):
@@ -379,16 +436,17 @@
     unit = (values * lax.rsqrt(jnp.sum(values * values, axis=1, keepdims=True) + EPSILON)).astype(
         jnp.bfloat16
     )
-    width = feature_dim // CHUNKS
-    parts = [unit[:, c * width : (c + 1) * width] for c in range(CHUNKS)]
 
     def exchange(part, count):
         return lax.all_to_all(
-            part.reshape(tile_rows, count, width), "tr", split_axis=0, concat_axis=0, tiled=True
-        ).reshape(tile_rows * count, width)
-
-    spread = permute(order % tile_rows * share + order // tile_rows, shard_rows, parts)
-    spread = [exchange(part, share) for part in spread]
+            part.reshape(tile_rows, count, feature_dim),
+            "tr",
+            split_axis=0,
+            concat_axis=0,
+            tiled=True,
+        ).reshape(tile_rows * count, feature_dim)
+
+    spread = placing(order % tile_rows * share + order // tile_rows, shard_rows)
 
     local = exclusive(column, 1)
     group_count = column.reshape(tile_rows, tile_rows, GROUP_CLUSTERS).sum(2)
@@ -409,8 +467,7 @@
     my_base = lax.dynamic_index_in_dim(base, me, 2, keepdims=False)
     lane = my_base[:, None, :] + number[:, :, None] // tile_rows
     target = jnp.sum(jnp.where(inside, via * capacity + lane, 0), axis=2).reshape(-1)
-    routed = permute(target, tile_rows * capacity, spread)
-    routed = [exchange(part, capacity) for part in routed]
+    route = placing(target, tile_rows * capacity)
 
     mine = lax.dynamic_slice_in_dim(column, me * GROUP_CLUSTERS, GROUP_CLUSTERS, 1)
     lengths = mine.T.reshape(-1)
@@ -420,30 +477,30 @@
         index[:, None] < (seg_start + lengths)[None, :]
     )
     number = index + jnp.sum(jnp.where(within, (seg_local - seg_start)[None, :], 0), axis=1)
-    route = number % tile_rows
+    way = number % tile_rows
     tables = lax.dynamic_index_in_dim(base, me, 1, keepdims=False)
     tables = jnp.tile(tables, (GROUP_CLUSTERS, 1))
     picked = jnp.sum(jnp.where(within[:, :, None], tables[None], 0), axis=1)
-    offset = jnp.sum(jnp.where(route[:, None] == via[None, :], picked, 0), axis=1)
-    source = route * capacity + offset + number // tile_rows
-    matrix = (
+    offset = jnp.sum(jnp.where(way[:, None] == via[None, :], picked, 0), axis=1)
+    source = way * capacity + offset + number // tile_rows
+    settle = (
         source[:, None] == jnp.arange(tile_rows * capacity, dtype=i32)[None, :]
     ).astype(jnp.bfloat16)
-    queries = [
-        jnp.dot(matrix, part, preferred_element_type=jnp.float32).astype(jnp.bfloat16)
-        for part in routed
-    ]
+
     totals = lax.dynamic_slice_in_dim(everywhere, me * GROUP_CLUSTERS, GROUP_CLUSTERS, 1)
     ends = jnp.cumsum(totals, axis=1)[:, : GROUP_CLUSTERS - 1]
     key_labels = jnp.sum((index[None, :, None] >= ends[:, None, :]).astype(i32), axis=2)
 
     if columns == 8:
-        back = plane_stats(queries[0], key_labels, place, tile_rows)
+        back = plane_stats(unit, spread, route, settle, key_labels, place, tile_rows)
         back = jnp.stack([back[:, 0].reshape(-1), back[:, 1].reshape(-1)])
     else:
-        keys = [lax.all_gather(part, "tc", axis=0, tiled=True) for part in queries]
+        landed = exchange(permute(spread, unit), share)
+        arrived = exchange(permute(route, landed), capacity)
+        queries = permute(settle, arrived)
+        keys = lax.all_gather(queries, "tc", axis=0, tiled=True)
         query_labels = lax.dynamic_index_in_dim(key_labels, place, 0, keepdims=False)
-        best, weighted = cluster_stats(queries, keys, query_labels, key_labels.reshape(-1), place)
+        best, weighted = cluster_stats([queries], [keys], query_labels, key_labels.reshape(-1), place)
         back = lax.all_gather(jnp.stack([best, weighted]), "tr", axis=1, tiled=True)
     shard_before = exclusive(column, 0)
     begin = exclusive(column.sum(0), 0) + lax.dynamic_index_in_dim(

time: 167 us -> 161 us (0.964)
  Pallas kernels: 63.3 us -> 143 us
  waiting for transfers between devices: 73 us -> 0 us
  starting transfers between devices: 8.27 us -> 0 us
  matrix products: 8.26 us -> 0.34 us
  other arithmetic: 9.19 us -> 11.9 us
    pallas_call x1, Pallas kernels: 50.5 us -> 130 us  [plane_stats(): pl.pallas_call(functools.partial(plane_kernel, tile_rows), in_specs=[vmem...]
    all_to_all x2 -> x0, waiting for transfers between devices: 73 us -> none  [exchange(): lax.all_to_all(part.reshape(tile_rows, count, width), 'tr', split_axis=0,...]
    all_to_all x2 -> x0, starting transfers between devices: 8.27 us -> none  [exchange(): lax.all_to_all(part.reshape(tile_rows, count, width), 'tr', split_axis=0,...]
    dot_general x3 -> x0, matrix products: 7.15 us -> none  [the longest x2 5.32 us: permute(): jnp.dot(matrix, part, preferred_element_type=jnp.float32)]
    convert_element_type x0 -> x4, other arithmetic: none -> 2.65 us  [the longest x1 1.47 us: per_device(): (values * lax.rsqrt(jnp.sum(values * values, axis=1, keepdims=True) + EPS...]
  transfers between devices with their start and end apart: 2 -> 0, of which waited for: 2 -> 0; matrix products, arithmetic and copies ran while one was open for 2% -> 0% of each run, Pallas kernels for 0% -> 0%
where the time goes in v3:
time: 161 us
  Pallas kernels  143 us (89%)
  other arithmetic  11.9 us (7%)
  local copies, waits for them, and re-layouts  4.52 us (3%)
    pallas_call x1, Pallas kernels, plane_stats(): pl.pallas_call(functools.partial(plane_kernel, tile_rows), in_specs=[vmem...  130 us
    pallas_call x1, Pallas kernels, gather_counts(): pl.pallas_call(functools.partial(count_kernel, rows, columns), in_specs=[...  12.8 us
    reduce_sum x1, other arithmetic, per_device(): mean_sim = jnp.sum(jnp.where(here, back[1][None, :], 0.0), axis=1)  3.27 us

profile of v3, /device:TPU:0, one launch (start us, length us, event | category | flops | bytes accessed | tf_op | source)
XLA Modules:
  0.0 160.8 jit_solution(11600911790149634905)
XLA Ops:
  0.7 0.8 convert_reduce_fusion.1
  1.6 0.6 scatter.4.held
  2.2 1.8 %fusion = f32[768]{0:T(1024)S(1)} fusion(bf16[768,1024]{1,0:T(8,128)(2,1)} %param.5), kind=kLoop, calls=%fused_computation.6 | loop fusion | flops 2358528 | bytes 1575936 | tf_op jit(solution)/shard_map/reduce_sum | solution.py:436
  4.0 0.3 fusion.7
  4.4 0.1 reduce.3
  4.6 12.8 %shard_map.58 = (s32[4,8,128]{2,1,0:T(8,128)}, s32[8,8,128]{2,1,0:T(8,128)}) custom-call(s32[8,128]{1,0:T(8,128)} %scatter.4.held), custom_call_target="tpu_custom_call" | custom-call | tf_op jit(solution)/shard_map/pallas_call | solution.py:170
  17.4 0.7 slice_reduce_fusion.1
  18.1 0.2 reduce-window_clone.1
  18.3 0.2 reduce_window_sum.70
  19.1 0.8 slice.32
  20.2 0.1 reduce.5
  20.5 0.1 reduce_sum.133
  20.6 0.2 reduce_window_sum.68
  21.4 0.1 copy.51
  22.3 0.6 gather_fusion
  22.9 0.3 copy.57.q_labels
  23.2 0.4 fusion.4.spread
  23.6 0.5 fusion.3.route
  24.1 0.3 fusion.2.settle
  24.4 0.6 copy-done
  25.0 1.5 fusion.1.unit
  26.5 130.4 %shard_map.59 = f32[4,8,768]{2,1,0:T(8,128)S(1)} custom-call(s32[2,768,1]{2,1,0:T(8,128)S(1)} %copy.57.q_labels, s32[6,3,1,256]{3,2,1,0:T(1,128)S(1)} %reshape.353.k_labels, bf16[768,1024]{1,0:T(8,128)(2,1)} %fusion.1.unit, bf16[768,768]{1,0:T(8,128)(2,1)S(1)} %fusion.4.spread, bf16[832,768]{1,0:T(8,128)(2,1)S(1)} %fusion.3.route, ...), custom_call_target="tpu_custom_call" | custom-call | tf_op jit(solution)/shard_map/pallas_call | solution.py:372
  156.9 3.3 %select_reduce_fusion = (f32[768]{0:T(1024)}, f32[768]{0:T(1024)S(1)}) fusion(f32[3072]{0:T(1024)S(1)} %bitcast.27, s32[768]{0:T(1024)S(1)} %get-tuple-element.36, f32[3072]{0:T(1024)S(1)} %bitcast.26), kind=kLoop, calls=%fused_computation.1 | loop fusion | flops 11794944 | bytes 33792 | tf_op jit(solution)/shard_map/reduce_sum | solution.py:512
  160.2 0.6 add_divide_fusion
  (54 shorter events, 2.6 us)
Async XLA Ops:
  0.6 3.3 %copy-start.1 = (s32[768]{0:T(1024)S(1)}, s32[768]{0:T(1024)}, u32[]{:S(2)}) copy-start(s32[768]{0:T(1024)} %param.6) | copy-start | bytes 9220
  23.6 1.4 copy-start
  160.2 0.6 copy-start.2

commit v4 on v3

--- a/solution.py
+++ b/solution.py
@@ -289,47 +289,48 @@
         if f:
             forward(f - 1)
 
-    def tile(side, qt, ks, kc, itself=False):
+    def strip(side, qt, ks, itself=False):
         q_rows = pl.ds(pl.multiple_of(qt * TILE, TILE), TILE)
-        k_rows = pl.ds(pl.multiple_of(kc * TILE, TILE), TILE)
         sims = lax.dot_general(
             blocks[2 * side, q_rows, :],
-            blocks[ks, k_rows, :],
+            blocks[ks],
             (((1,), (1,)), ((), ())),
             preferred_element_type=jnp.float32,
         )
-        mask = q_labels[side, q_rows, :] == k_labels[ks, kc]
+        mask = q_labels[side, q_rows, :] == k_labels[ks]
         if itself:
-            row = lax.broadcasted_iota(jnp.int32, (TILE, TILE), 0) + qt * TILE
-            col = lax.broadcasted_iota(jnp.int32, (TILE, TILE), 1) + kc * TILE
+            row = lax.broadcasted_iota(jnp.int32, (TILE, rows), 0) + qt * TILE
+            col = lax.broadcasted_iota(jnp.int32, (TILE, rows), 1)
             mask = mask & (row != col)
         sims = jnp.where(mask, sims, NEGATIVE)
-        left, right = sims[:, :128], sims[:, 128:]
+        pieces = [sims[:, n * 128 : (n + 1) * 128] for n in range(rows // 128)]
         old = stats[side, 0, q_rows, :]
-        top = jnp.maximum(old, jnp.maximum(left, right))
+        top = functools.reduce(jnp.maximum, pieces, old)
         factor = jnp.exp(SCALE * (old - top))
-        left_term = jnp.exp(SCALE * (left - top))
-        right_term = jnp.exp(SCALE * (right - top))
+        total = stats[side, 1, q_rows, :] * factor
+        weight = stats[side, 2, q_rows, :] * factor
+        for piece in pieces:
+            term = jnp.exp(SCALE * (piece - top))
+            total = total + term
+            weight = weight + term * piece
         stats[side, 0, q_rows, :] = top
-        stats[side, 1, q_rows, :] = stats[side, 1, q_rows, :] * factor + (left_term + right_term)
-        stats[side, 2, q_rows, :] = stats[side, 2, q_rows, :] * factor + (
-            left_term * left + right_term * right
-        )
-
-    def each(count, body):
-        lax.fori_loop(0, count, lambda i, none: (body(i), none)[1], 0)
-
-    square = tiles * tiles
-    each(square, lambda i: tile(0, i // tiles, 0, i % tiles, itself=True))
+        stats[side, 1, q_rows, :] = total
+        stats[side, 2, q_rows, :] = weight
+
+    def each(body):
+        lax.fori_loop(0, tiles, lambda i, none: (body(i), none)[1], 0, unroll=True)
+
+    each(lambda i: strip(0, i, 0, itself=True))
     forward(pieces - 1)
     for copy in from_sibling:
         copy.wait()
-    each(square, lambda i: tile(0, i // tiles, 1, i % tiles))
-    each(2 * square, lambda i: tile(0, i // 2 % tiles, 2 + i % 2, i // 2 // tiles))
-    each(square, lambda i: tile(1, i // tiles, 3, i % tiles))
+    each(lambda i: strip(0, i, 1))
+    each(lambda i: strip(0, i, 2))
+    each(lambda i: strip(0, i, 3))
+    each(lambda i: strip(1, i, 3))
     for copy in passed:
         copy.wait()
-    each(square, lambda i: tile(1, i // tiles, 5, i % tiles))
+    each(lambda i: strip(1, i, 5))
 
     def fold(side):
         top = stats[side, 0]
@@ -343,7 +344,8 @@
 
     part[1] = fold(1)
     diagonal = send(part.at[1], theirs, peers[1])
-    each(2 * square, lambda i: tile(0, i // 2 % tiles, 4 + i % 2, i // 2 // tiles))
+    each(lambda i: strip(0, i, 4))
+    each(lambda i: strip(0, i, 5))
     mine = fold(0)
     diagonal.wait()
     other = theirs[...]
@@ -390,7 +392,7 @@
         ),
     )(
         near[jnp.array([0, 2])][:, :, None],
-        near.reshape(6, tiles, 1, TILE),
+        near[:, None, :],
         unit,
         spread,
         route,

time: 161 us -> 149 us (0.925)
  Pallas kernels: 143 us -> 131 us
    pallas_call x1, Pallas kernels: 130 us -> 118 us  [plane_stats(): pl.pallas_call(functools.partial(plane_kernel, tile_rows), in_specs=[vmem...]
where the time goes in v4:
time: 149 us
  Pallas kernels  131 us (88%)
  other arithmetic  12.1 us (8%)
  local copies, waits for them, and re-layouts  4.51 us (3%)
    pallas_call x1, Pallas kernels, plane_stats(): pl.pallas_call(functools.partial(plane_kernel, tile_rows), in_specs=[vmem...  118 us
    pallas_call x1, Pallas kernels, gather_counts(): pl.pallas_call(functools.partial(count_kernel, rows, columns), in_specs=[...  12.8 us
    reduce_sum x1, other arithmetic, per_device(): mean_sim = jnp.sum(jnp.where(here, back[1][None, :], 0.0), axis=1)  3.49 us

profile of v4, /device:TPU:0, one launch (start us, length us, event | category | flops | bytes accessed | tf_op | source)
XLA Modules:
  0.0 148.5 jit_solution(14557473270466355187)
XLA Ops:
  0.7 0.8 convert_reduce_fusion.1
  1.6 0.6 scatter.4.held
  2.2 1.8 %fusion = f32[768]{0:T(1024)S(1)} fusion(bf16[768,1024]{1,0:T(8,128)(2,1)} %param.5), kind=kLoop, calls=%fused_computation.6 | loop fusion | flops 2358528 | bytes 1575936 | tf_op jit(solution)/shard_map/reduce_sum | solution.py:438
  4.0 0.3 fusion.7
  4.4 0.1 reduce.3
  4.6 12.8 %shard_map.58 = (s32[4,8,128]{2,1,0:T(8,128)}, s32[8,8,128]{2,1,0:T(8,128)}) custom-call(s32[8,128]{1,0:T(8,128)} %scatter.4.held), custom_call_target="tpu_custom_call" | custom-call | tf_op jit(solution)/shard_map/pallas_call | solution.py:170
  17.4 0.7 slice_reduce_fusion.1
  18.1 0.2 reduce-window_clone.1
  18.3 0.2 reduce_window_sum.70
  19.1 0.8 slice.32
  20.2 0.1 reduce.5
  20.5 0.1 reduce_sum.133
  20.6 0.2 reduce_window_sum.68
  21.4 0.1 copy.51
  22.3 0.6 gather_fusion
  22.9 0.3 copy.57.q_labels
  23.2 0.4 fusion.4.spread
  23.6 0.5 fusion.3.route
  24.1 0.3 fusion.2.settle
  24.4 0.6 copy-done
  25.0 1.5 fusion.1.unit
  26.5 117.9 %shard_map.59 = f32[4,8,768]{2,1,0:T(8,128)S(1)} custom-call(s32[2,768,1]{2,1,0:T(8,128)S(1)} %copy.57.q_labels, s32[6,1,768]{2,1,0:T(1,128)S(1)} %broadcast_in_dim.132.k_labels, bf16[768,1024]{1,0:T(8,128)(2,1)} %fusion.1.unit, bf16[768,768]{1,0:T(8,128)(2,1)S(1)} %fusion.4.spread, bf16[832,768]{1,0:T(8,128)(2,1)S(1)} %fusion.3.route, ...), custom_call_target="tpu_custom_call" | custom-call | tf_op jit(solution)/shard_map/pallas_call | solution.py:374
  144.4 3.5 %select_reduce_fusion = (f32[768]{0:T(1024)}, f32[768]{0:T(1024)S(1)}) fusion(f32[3072]{0:T(1024)S(1)} %bitcast.27, s32[768]{0:T(1024)S(1)} %get-tuple-element.36, f32[3072]{0:T(1024)S(1)} %bitcast.26), kind=kLoop, calls=%fused_computation.1 | loop fusion | flops 11794944 | bytes 33792 | tf_op jit(solution)/shard_map/reduce_sum | solution.py:514
  147.9 0.6 add_divide_fusion
  (54 shorter events, 2.6 us)
Async XLA Ops:
  0.6 3.3 %copy-start.1 = (s32[768]{0:T(1024)S(1)}, s32[768]{0:T(1024)}, u32[]{:S(2)}) copy-start(s32[768]{0:T(1024)} %param.6) | copy-start | bytes 9220
  23.6 1.4 copy-start
  147.9 0.6 copy-start.2
